TPU v7x, 32 devices: a whole 2x2x4 slice. The times are simulated.
32 devices in a mesh: rhs: 4 (over y, x), rows: 8 (over z, core).
Axes of the slice: x: 2, y: 2, z: 4, core: 2. Of those that a mesh axis runs over, the one named last changes fastest.
Arguments:
- right_side: float32 [16384, 512], P('rows', 'rhs'), may hold values from -6 to 6
- fine_blocks: bfloat16 [128, 32, 128, 128], P('rows'), may hold values from -0.09375 to 0.09375
- fine_columns: int32 [128, 32], P('rows'), may hold values from 0 to 127, as said below
- fine_diag: float32 [16384], P('rows'), may hold values from 3 to 6
- aggregate: int32 [128], P('rows'), may hold values from 0 to 31, as said below
- coarse_blocks: float32 [32, 3, 128, 128], P(('rhs', 'rows')), may hold values from -0.3125 to 0.3125
- coarse_diag: float32 [4096], P(('rhs', 'rows')), may hold values from 1 to 2
Outputs:
- solution: float32 [16384, 512], P('rows', 'rhs')
Inputs may be any that keep to these rules, and one draw needn't show every extreme that they name: `fine_columns`: the 32 stored blocks of fine block-row r have 32 distinct columns, each equal to r + o modulo 128 for an offset o from -16 to 16, and every row holds both end offsets. `aggregate`: fine block-row r maps to a coarse block c with c % (8) equal to r // 16; every coarse block receives one or more fine block-rows.
All inputs are finite; a program needn't handle non-finite values.
Results may differ from a plain program's by a relative error of at most 0.004.
Values may be sent and summed in bfloat16 or wider, within the bound.
A program may use at most 128 MiB of HBM per device.

v0:
```python
import jax
import jax.numpy as jnp
from jax import lax
from jax.sharding import PartitionSpec as P

CYCLES = 2
SWEEPS = 2
CHEB = 3


relax_weight = 0.7
centre = 1.0
half_width = 0.6


def with_halo(cells, sides, width):
    for axis, dim in sides:
        count = lax.axis_size(axis)
        head = lax.slice_in_dim(cells, 0, width, axis=dim)
        tail = lax.slice_in_dim(cells, cells.shape[dim] - width, cells.shape[dim], axis=dim)
        cells = jnp.concatenate(
            [
                lax.ppermute(tail, axis, [(i, (i + 1) % count) for i in range(count)]),
                cells,
                lax.ppermute(head, axis, [((i + 1) % count, i) for i in range(count)]),
            ],
            axis=dim,
        )
    return cells


def fine_apply(field, fine_blocks, fine_columns, fine_scale):
    block_rows = fine_blocks.shape[0]
    reach = fine_blocks.shape[1] // 2
    total_blocks = block_rows * lax.axis_size("rows")
    rounded = field.astype(jnp.bfloat16)
    extended = with_halo(rounded, (("rows", 0),), reach)
    first_block = lax.axis_index("rows") * block_rows - reach
    local_index = jnp.mod(fine_columns - first_block, total_blocks)
    gathered = extended[local_index]
    product = jnp.einsum(
        "rkij,rkjn->rin", fine_blocks, gathered, preferred_element_type=jnp.float32
    )
    return fine_scale * field + product


def coarse_terms(field, lower_rim, upper_rim, coarse_ops, coarse_scale):
    high = lax.Precision.HIGHEST
    total = coarse_scale * field
    total = total + jnp.einsum(
        "qij,qjn->qin",
        coarse_ops[:, 0],
        lower_rim,
        precision=high,
        preferred_element_type=jnp.float32,
    )
    total = total + jnp.einsum(
        "qij,qjn->qin", coarse_ops[:, 1], field, precision=high, preferred_element_type=jnp.float32
    )
    total = total + jnp.einsum(
        "qij,qjn->qin",
        coarse_ops[:, 2],
        upper_rim,
        precision=high,
        preferred_element_type=jnp.float32,
    )
    return total


def spread_apply(field, coarse_ops, coarse_scale):
    block_size = field.shape[1]
    extended = with_halo(field.astype(jnp.bfloat16), (("rows", 1),), block_size).astype(field.dtype)
    lower_rim = extended[:, :block_size]
    upper_rim = extended[:, 2 * block_size :]
    empty = jnp.zeros((1,) + field.shape[1:], jnp.float32)
    device_pos = lax.axis_index("rows")
    row_devices = lax.axis_size("rows")
    lower_rim = jnp.where(
        device_pos == 0, jnp.concatenate([empty, lower_rim[:-1]], axis=0), lower_rim
    )
    upper_rim = jnp.where(
        device_pos == row_devices - 1, jnp.concatenate([upper_rim[1:], empty], axis=0), upper_rim
    )
    return coarse_terms(field, lower_rim, upper_rim, coarse_ops, coarse_scale)


def chebyshev(source, operator_fn, coarse_ops, coarse_scale):
    sigma_ratio = centre / half_width
    ratio_old = 1.0 / sigma_ratio
    update = source / coarse_scale / centre
    correction = update
    for step_index in range(CHEB - 1):
        ratio_new = 1.0 / (2.0 * sigma_ratio - ratio_old)
        scaled = (source - operator_fn(correction, coarse_ops, coarse_scale)) / coarse_scale
        update = ratio_new * ratio_old * update + 2.0 * ratio_new / half_width * scaled
        correction = correction + update
        ratio_old = ratio_new
    return correction


def shards(right_side, fine_blocks, fine_columns, fine_diag, aggregate, coarse_blocks, coarse_diag):
    block_rows = fine_blocks.shape[0]
    block_size = fine_blocks.shape[2]
    width_rhs = right_side.shape[1]
    groups = lax.axis_size("rhs")
    row_devices = lax.axis_size("rows")
    source = right_side.reshape(block_rows, block_size, width_rhs)
    fine_scale = fine_diag.reshape(block_rows, block_size, 1)
    group_id = aggregate // row_devices
    selector = (group_id[None, :] == jnp.arange(groups, dtype=jnp.int32)[:, None]).astype(
        jnp.float32
    )
    spread_ops, spread_diag = (
        lax.all_gather(coarse_blocks.astype(jnp.bfloat16), "rhs", axis=0, tiled=True).astype(
            coarse_blocks.dtype
        ),
        lax.all_gather(coarse_diag.astype(jnp.bfloat16), "rhs", axis=0, tiled=True).astype(
            coarse_diag.dtype
        ),
    )
    spread_scale = spread_diag.reshape(groups, block_size, 1)
    solution = jnp.zeros((block_rows, block_size, width_rhs), jnp.float32)
    for turn_index in range(CYCLES):
        for sweep_index in range(SWEEPS):
            if turn_index == 0 and sweep_index == 0:
                solution = relax_weight * source / fine_scale
            else:
                solution = (
                    solution
                    + relax_weight
                    * (source - fine_apply(solution, fine_blocks, fine_columns, fine_scale))
                    / fine_scale
                )
        residual = source - fine_apply(solution, fine_blocks, fine_columns, fine_scale)
        coarse_side = jnp.einsum(
            "qf,fin->qin",
            selector,
            residual,
            precision=lax.Precision.HIGHEST,
            preferred_element_type=jnp.float32,
        )
        correction = chebyshev(coarse_side, spread_apply, spread_ops, spread_scale)
        prolonged = jnp.einsum(
            "qf,qin->fin",
            selector,
            correction,
            precision=lax.Precision.HIGHEST,
            preferred_element_type=jnp.float32,
        )
        solution = solution + prolonged
        for sweep_index in range(SWEEPS):
            solution = (
                solution
                + relax_weight
                * (source - fine_apply(solution, fine_blocks, fine_columns, fine_scale))
                / fine_scale
            )
    return solution.reshape(block_rows * block_size, width_rhs)


def solution(mesh):
    in_specs = (
        P("rows", "rhs"),
        P("rows", None, None, None),
        P("rows", None),
        P("rows"),
        P("rows"),
        P(("rhs", "rows"), None, None, None),
        P(("rhs", "rows")),
    )
    out_specs = P("rows", "rhs")
    return jax.shard_map(shards, mesh=mesh, in_specs=in_specs, out_specs=out_specs, check_vma=False)
```

profile of v0, /device:TPU:1, one launch (start us, length us, event | category | flops | bytes accessed | tf_op | source)
XLA Modules:
  0.0 445.0 jit_solution(4240846690875907494)
XLA Ops:
  15.3 13.9 %gather_fusion = bf16[512,128,128]{2,1,0:T(8,128)(2,1)} fusion(bf16[48,128,128]{2,1,0:T(8,128)(2,1)S(1)} %pad_maximum_fusion, s32[1024]{0:T(1024)S(1)} %pad_clamp_fusion), kind=kCustom, calls=%fused_computation | custom fusion | bytes 33556480 | tf_op jit(solution)/shard_map/gather | solution.py:40
  29.3 16.1 %fusion.114 = (bf16[16,128,128]{2,1,0:T(8,128)(2,1)S(1)}, f32[16,128,128]{2,1,0:T(8,128)}) fusion(f32[16,128,128]{2,1,0:T(8,128)S(1)} %bitcast.288, bf16[16,32,128,128]{3,2,1,0:T(8,128)(2,1)} %param.8, bf16[16,32,128,128]{3,2,1,0:T(8,128)(2,1)} %bitcast.286, f32[16,128]{1,0:T(8,128)S(1)} %bitcast.298), kind=kOutput, calls=%fused_computation.181 | convolution fusion | flops 2149842944 | bytes 36184064 | tf_op jit(solution)/shard_map/rkij,rkjn->rin/dot_general | solution.py:41
  62.9 13.9 %gather_fusion.1 = bf16[512,128,128]{2,1,0:T(8,128)(2,1)} fusion(bf16[48,128,128]{2,1,0:T(8,128)(2,1)S(1)} %pad_maximum_fusion.1, s32[1024]{0:T(1024)S(1)} %pad_clamp_fusion), kind=kCustom, calls=%fused_computation.1 | custom fusion | bytes 33556480 | tf_op jit(solution)/shard_map/gather | solution.py:40
  76.9 16.3 %fusion.4 = f32[16,128,128]{2,1,0:T(8,128)} fusion(f32[16,128,128]{2,1,0:T(8,128)S(1)} %bitcast.289, bf16[16,32,128,128]{3,2,1,0:T(8,128)(2,1)} %param.8, bf16[16,32,128,128]{3,2,1,0:T(8,128)(2,1)} %bitcast.278, f32[16,128,128]{2,1,0:T(8,128)} %get-tuple-element.32, f32[16,128]{1,0:T(8,128)S(1)} %bitcast.299), kind=kOutput, calls=%fused_computation.31 | convolution fusion | flops 2148270080 | bytes 36708352 | tf_op jit(solution)/shard_map/rkij,rkjn->rin/dot_general | solution.py:41
  133.1 13.9 %gather_fusion.2 = bf16[512,128,128]{2,1,0:T(8,128)(2,1)} fusion(bf16[48,128,128]{2,1,0:T(8,128)(2,1)S(1)} %pad_maximum_fusion.2, s32[1024]{0:T(1024)S(1)} %pad_clamp_fusion), kind=kCustom, calls=%fused_computation.2 | custom fusion | bytes 33556480 | tf_op jit(solution)/shard_map/gather | solution.py:40
  147.0 14.6 %fusion.115 = (bf16[16,128,128]{2,1,0:T(8,128)(2,1)S(1)}, f32[16,128,128]{2,1,0:T(8,128)}) fusion(f32[16,128,128]{2,1,0:T(8,128)S(1)} %bitcast.290, bf16[16,32,128,128]{3,2,1,0:T(8,128)(2,1)} %param.8, bf16[16,32,128,128]{3,2,1,0:T(8,128)(2,1)} %bitcast.280, f32[16,128]{1,0:T(8,128)S(1)} %bitcast.300, f32[16,128,128]{2,1,0:T(8,128)} %get-tuple-element.32, ...), kind=kOutput, calls=%fused_computation.182 | convolution fusion | flops 2149580800 | bytes 38281216 | tf_op jit(solution)/shard_map/rkij,rkjn->rin/dot_general | solution.py:41
  163.5 12.4 %collective-permute-done.11 = bf16[16,128,128]{2,1,0:T(8,128)(2,1)S(1)} collective-permute-done((bf16[16,128,128]{2,1,0:T(8,128)(2,1)S(1)}, bf16[16,128,128]{2,1,0:T(8,128)(2,1)S(1)}, u32[]{:S(2)}, u32[]{:S(2)}) %collective-permute-start.11) | collective-permute-done | bytes 524320 | tf_op jit(solution)/shard_map/ppermute | solution.py:25
  176.0 13.9 %gather_fusion.3 = bf16[512,128,128]{2,1,0:T(8,128)(2,1)} fusion(bf16[48,128,128]{2,1,0:T(8,128)(2,1)S(1)} %pad_maximum_fusion.3, s32[1024]{0:T(1024)S(1)} %pad_clamp_fusion), kind=kCustom, calls=%fused_computation.3 | custom fusion | bytes 33556480 | tf_op jit(solution)/shard_map/gather | solution.py:40
  189.9 14.1 %fusion.116 = (bf16[16,128,128]{2,1,0:T(8,128)(2,1)S(1)}, f32[16,128,128]{2,1,0:T(8,128)}) fusion(f32[16,128,128]{2,1,0:T(8,128)} %get-tuple-element.35, f32[16,128,128]{2,1,0:T(8,128)S(1)} %bitcast.291, bf16[16,32,128,128]{3,2,1,0:T(8,128)(2,1)} %param.8, bf16[16,32,128,128]{3,2,1,0:T(8,128)(2,1)} %bitcast.281, f32[16,128]{1,0:T(8,128)S(1)} %bitcast.301), kind=kOutput, calls=%fused_computation.183 | convolution fusion | flops 2149318656 | bytes 37232640 | tf_op jit(solution)/shard_map/rkij,rkjn->rin/dot_general | solution.py:41
  205.8 12.5 %collective-permute-done.13 = bf16[16,128,128]{2,1,0:T(8,128)(2,1)S(1)} collective-permute-done((bf16[16,128,128]{2,1,0:T(8,128)(2,1)S(1)}, bf16[16,128,128]{2,1,0:T(8,128)(2,1)S(1)}, u32[]{:S(2)}, u32[]{:S(2)}) %collective-permute-start.13) | collective-permute-done | bytes 524320 | tf_op jit(solution)/shard_map/ppermute | solution.py:25
  218.4 13.9 %gather_fusion.4 = bf16[512,128,128]{2,1,0:T(8,128)(2,1)} fusion(bf16[48,128,128]{2,1,0:T(8,128)(2,1)S(1)} %pad_maximum_fusion.4, s32[1024]{0:T(1024)S(1)} %pad_clamp_fusion), kind=kCustom, calls=%fused_computation.4 | custom fusion | bytes 33556480 | tf_op jit(solution)/shard_map/gather | solution.py:40
  232.4 14.1 %fusion.117 = (bf16[16,128,128]{2,1,0:T(8,128)(2,1)S(1)}, f32[16,128,128]{2,1,0:T(8,128)}) fusion(f32[16,128,128]{2,1,0:T(8,128)} %get-tuple-element.37, f32[16,128,128]{2,1,0:T(8,128)S(1)} %bitcast.292, bf16[16,32,128,128]{3,2,1,0:T(8,128)(2,1)} %param.8, bf16[16,32,128,128]{3,2,1,0:T(8,128)(2,1)} %bitcast.282, f32[16,128]{1,0:T(8,128)S(1)} %bitcast.302), kind=kOutput, calls=%fused_computation.184 | convolution fusion | flops 2149318656 | bytes 37232640 | tf_op jit(solution)/shard_map/rkij,rkjn->rin/dot_general | solution.py:41
  248.4 12.3 %collective-permute-done.15 = bf16[16,128,128]{2,1,0:T(8,128)(2,1)S(1)} collective-permute-done((bf16[16,128,128]{2,1,0:T(8,128)(2,1)S(1)}, bf16[16,128,128]{2,1,0:T(8,128)(2,1)S(1)}, u32[]{:S(2)}, u32[]{:S(2)}) %collective-permute-start.15) | collective-permute-done | bytes 524320 | tf_op jit(solution)/shard_map/ppermute | solution.py:25
  260.9 13.9 %gather_fusion.5 = bf16[512,128,128]{2,1,0:T(8,128)(2,1)} fusion(bf16[48,128,128]{2,1,0:T(8,128)(2,1)S(1)} %pad_maximum_fusion.5, s32[1024]{0:T(1024)S(1)} %pad_clamp_fusion), kind=kCustom, calls=%fused_computation.5 | custom fusion | bytes 33556480 | tf_op jit(solution)/shard_map/gather | solution.py:40
  274.8 14.1 %fusion.118 = (bf16[16,128,128]{2,1,0:T(8,128)(2,1)S(1)}, f32[16,128,128]{2,1,0:T(8,128)}) fusion(f32[16,128,128]{2,1,0:T(8,128)} %get-tuple-element.39, f32[16,128,128]{2,1,0:T(8,128)S(1)} %bitcast.293, bf16[16,32,128,128]{3,2,1,0:T(8,128)(2,1)} %param.8, bf16[16,32,128,128]{3,2,1,0:T(8,128)(2,1)} %bitcast.283, f32[16,128]{1,0:T(8,128)S(1)} %bitcast.303), kind=kOutput, calls=%fused_computation.185 | convolution fusion | flops 2149318656 | bytes 37232640 | tf_op jit(solution)/shard_map/rkij,rkjn->rin/dot_general | solution.py:41
  290.6 12.5 %collective-permute-done.17 = bf16[16,128,128]{2,1,0:T(8,128)(2,1)S(1)} collective-permute-done((bf16[16,128,128]{2,1,0:T(8,128)(2,1)S(1)}, bf16[16,128,128]{2,1,0:T(8,128)(2,1)S(1)}, u32[]{:S(2)}, u32[]{:S(2)}) %collective-permute-start.17) | collective-permute-done | bytes 524320 | tf_op jit(solution)/shard_map/ppermute | solution.py:25
  303.3 13.9 %gather_fusion.6 = bf16[512,128,128]{2,1,0:T(8,128)(2,1)} fusion(bf16[48,128,128]{2,1,0:T(8,128)(2,1)S(1)} %pad_maximum_fusion.6, s32[1024]{0:T(1024)S(1)} %pad_clamp_fusion), kind=kCustom, calls=%fused_computation.6 | custom fusion | bytes 33556480 | tf_op jit(solution)/shard_map/gather | solution.py:40
  317.2 16.3 %fusion.18 = f32[16,128,128]{2,1,0:T(8,128)} fusion(f32[16,128,128]{2,1,0:T(8,128)S(1)} %bitcast.294, bf16[16,32,128,128]{3,2,1,0:T(8,128)(2,1)} %param.8, bf16[16,32,128,128]{3,2,1,0:T(8,128)(2,1)} %bitcast.279, f32[16,128,128]{2,1,0:T(8,128)} %get-tuple-element.41, f32[16,128]{1,0:T(8,128)S(1)} %bitcast.304), kind=kOutput, calls=%fused_computation.45 | convolution fusion | flops 2148270080 | bytes 36708352 | tf_op jit(solution)/shard_map/rkij,rkjn->rin/dot_general | solution.py:41
  359.6 11.9 %collective-permute-done.23 = bf16[16,128,128]{2,1,0:T(8,128)(2,1)S(1)} collective-permute-done((bf16[16,128,128]{2,1,0:T(8,128)(2,1)S(1)}, bf16[16,128,128]{2,1,0:T(8,128)(2,1)S(1)}, u32[]{:S(2)}, u32[]{:S(2)}) %collective-permute-start.23) | collective-permute-done | bytes 524320 | tf_op jit(solution)/shard_map/ppermute | solution.py:25
  371.6 13.9 %gather_fusion.7 = bf16[512,128,128]{2,1,0:T(8,128)(2,1)} fusion(bf16[48,128,128]{2,1,0:T(8,128)(2,1)S(1)} %pad_maximum_fusion.7, s32[1024]{0:T(1024)S(1)} %pad_clamp_fusion), kind=kCustom, calls=%fused_computation.7 | custom fusion | bytes 33556480 | tf_op jit(solution)/shard_map/gather | solution.py:40
  385.6 14.6 %fusion.119 = (bf16[16,128,128]{2,1,0:T(8,128)(2,1)S(1)}, f32[16,128,128]{2,1,0:T(8,128)}) fusion(f32[16,128,128]{2,1,0:T(8,128)S(1)} %bitcast.295, bf16[16,32,128,128]{3,2,1,0:T(8,128)(2,1)} %param.8, bf16[16,32,128,128]{3,2,1,0:T(8,128)(2,1)} %bitcast.284, f32[16,128]{1,0:T(8,128)S(1)} %bitcast.305, f32[16,128,128]{2,1,0:T(8,128)} %get-tuple-element.41, ...), kind=kOutput, calls=%fused_computation.186 | convolution fusion | flops 2149580800 | bytes 38281216 | tf_op jit(solution)/shard_map/rkij,rkjn->rin/dot_general | solution.py:41
  402.0 12.3 %collective-permute-done.25 = bf16[16,128,128]{2,1,0:T(8,128)(2,1)S(1)} collective-permute-done((bf16[16,128,128]{2,1,0:T(8,128)(2,1)S(1)}, bf16[16,128,128]{2,1,0:T(8,128)(2,1)S(1)}, u32[]{:S(2)}, u32[]{:S(2)}) %collective-permute-start.25) | collective-permute-done | bytes 524320 | tf_op jit(solution)/shard_map/ppermute | solution.py:25
  414.5 13.9 %gather_fusion.8 = bf16[512,128,128]{2,1,0:T(8,128)(2,1)} fusion(bf16[48,128,128]{2,1,0:T(8,128)(2,1)S(1)} %pad_maximum_fusion.8, s32[1024]{0:T(1024)S(1)} %pad_clamp_fusion), kind=kCustom, calls=%fused_computation.8 | custom fusion | bytes 33556480 | tf_op jit(solution)/shard_map/gather | solution.py:40
  428.5 16.3 %fusion.26 = f32[16,128,128]{2,1,0:T(8,128)} fusion(f32[16,128,128]{2,1,0:T(8,128)} %get-tuple-element.44, f32[16,128,128]{2,1,0:T(8,128)S(1)} %bitcast.296, bf16[16,32,128,128]{3,2,1,0:T(8,128)(2,1)} %param.8, bf16[16,32,128,128]{3,2,1,0:T(8,128)(2,1)} %bitcast.285, f32[16,128]{1,0:T(8,128)S(1)} %bitcast.306), kind=kOutput, calls=%fused_computation.53 | convolution fusion | flops 2149056512 | bytes 36708352 | tf_op jit(solution)/shard_map/rkij,rkjn->rin/dot_general | solution.py:41
  (126 shorter events, 108.7 us)
Async XLA Ops:
  1.6 10.8 %collective-permute-start.1 = (bf16[16,128,128]{2,1,0:T(8,128)(2,1)S(1)}, bf16[16,128,128]{2,1,0:T(8,128)(2,1)S(1)}, u32[]{:S(2)}, u32[]{:S(2)}) collective-permute-start(bf16[16,128,128]{2,1,0:T(8,128)(2,1)S(1)} %fusion.43), channel_id=1, source_target_pairs={{1,0},{2,1},{3,2},{4,3},{5,4},{6,5},{7,6},{0,7},{9,8},{10,9},{11,1... | collective-permute-start | bytes 1572872 | tf_op jit(solution)/shard_map/ppermute | solution.py:25
  1.7 12.4 %collective-permute-start = (bf16[16,128,128]{2,1,0:T(8,128)(2,1)S(1)}, bf16[16,128,128]{2,1,0:T(8,128)(2,1)}, u32[]{:S(2)}, u32[]{:S(2)}) collective-permute-start(bf16[16,128,128]{2,1,0:T(8,128)(2,1)S(1)} %fusion.43), channel_id=1, source_target_pairs={{0,1},{1,2},{2,3},{3,4},{4,5},{5,6},{6,7},{7,0},{8,9},{9,10},{10,1... | collective-permute-start | bytes 1572872 | tf_op jit(solution)/shard_map/ppermute | solution.py:23
  45.4 13.7 %collective-permute-start.3 = (bf16[16,128,128]{2,1,0:T(8,128)(2,1)S(1)}, bf16[16,128,128]{2,1,0:T(8,128)(2,1)S(1)}, u32[]{:S(2)}, u32[]{:S(2)}) collective-permute-start(bf16[16,128,128]{2,1,0:T(8,128)(2,1)S(1)} %get-tuple-element.31), channel_id=1, source_target_pairs={{1,0},{2,1},{3,2},{4,3},{5,4},{6,5},{7,6},{0,7},{9,8},{10,9},{11,1... | collective-permute-start | bytes 1572872 | tf_op jit(solution)/shard_map/ppermute | solution.py:25
  51.0 10.8 %collective-permute-start.2 = (bf16[16,128,128]{2,1,0:T(8,128)(2,1)S(1)}, bf16[16,128,128]{2,1,0:T(8,128)(2,1)S(1)}, u32[]{:S(2)}, u32[]{:S(2)}) collective-permute-start(bf16[16,128,128]{2,1,0:T(8,128)(2,1)S(1)} %get-tuple-element.31), channel_id=1, source_target_pairs={{0,1},{1,2},{2,3},{3,4},{4,5},{5,6},{6,7},{7,0},{8,9},{9,10},{10,1... | collective-permute-start | bytes 1572872 | tf_op jit(solution)/shard_map/ppermute | solution.py:23
  95.6 5.2 %collective-permute-start.5 = (bf16[4,128,128]{2,0,1:T(4,128)(2,1)S(1)}, bf16[4,128,128]{2,0,1:T(4,128)(2,1)S(1)}, u32[]{:S(2)}, u32[]{:S(2)}) collective-permute-start(bf16[4,128,128]{2,0,1:T(4,128)(2,1)S(1)} %get-tuple-element.13), channel_id=1, source_target_pairs={{1,0},{2,1},{3,2},{4,3},{5,4},{6,5},{7,6},{0,7},{9,8},{10,9},{11,1... | collective-permute-start | bytes 393224 | tf_op jit(solution)/shard_map/ppermute | solution.py:25
  104.1 7.1 %collective-permute-start.7 = (bf16[4,128,128]{2,0,1:T(4,128)(2,1)S(1)}, bf16[4,128,128]{2,0,1:T(4,128)(2,1)S(1)}, u32[]{:S(2)}, u32[]{:S(2)}) collective-permute-start(bf16[4,128,128]{2,0,1:T(4,128)(2,1)S(1)} %get-tuple-element.10), channel_id=1, source_target_pairs={{1,0},{2,1},{3,2},{4,3},{5,4},{6,5},{7,6},{0,7},{9,8},{10,9},{11,1... | collective-permute-start | bytes 393224 | tf_op jit(solution)/shard_map/ppermute | solution.py:25
  109.5 3.5 collective-permute-start.6
  117.9 15.0 %collective-permute-start.9 = (bf16[16,128,128]{2,1,0:T(8,128)(2,1)S(1)}, bf16[16,128,128]{2,1,0:T(8,128)(2,1)S(1)}, u32[]{:S(2)}, u32[]{:S(2)}) collective-permute-start(bf16[16,128,128]{2,1,0:T(8,128)(2,1)S(1)} %fusion.44), channel_id=1, source_target_pairs={{1,0},{2,1},{3,2},{4,3},{5,4},{6,5},{7,6},{0,7},{9,8},{10,9},{11,1... | collective-permute-start | bytes 1572872 | tf_op jit(solution)/shard_map/ppermute | solution.py:25
  121.1 11.8 %collective-permute-start.8 = (bf16[16,128,128]{2,1,0:T(8,128)(2,1)S(1)}, bf16[16,128,128]{2,1,0:T(8,128)(2,1)S(1)}, u32[]{:S(2)}, u32[]{:S(2)}) collective-permute-start(bf16[16,128,128]{2,1,0:T(8,128)(2,1)S(1)} %fusion.44), channel_id=1, source_target_pairs={{0,1},{1,2},{2,3},{3,4},{4,5},{5,6},{6,7},{7,0},{8,9},{9,10},{10,1... | collective-permute-start | bytes 1572872 | tf_op jit(solution)/shard_map/ppermute | solution.py:23
  161.6 14.3 %collective-permute-start.11 = (bf16[16,128,128]{2,1,0:T(8,128)(2,1)S(1)}, bf16[16,128,128]{2,1,0:T(8,128)(2,1)S(1)}, u32[]{:S(2)}, u32[]{:S(2)}) collective-permute-start(bf16[16,128,128]{2,1,0:T(8,128)(2,1)S(1)} %get-tuple-element.34), channel_id=1, source_target_pairs={{1,0},{2,1},{3,2},{4,3},{5,4},{6,5},{7,6},{0,7},{9,8},{10,9},{11,1... | collective-permute-start | bytes 1572872 | tf_op jit(solution)/shard_map/ppermute | solution.py:25
  162.0 13.9 %collective-permute-start.10 = (bf16[16,128,128]{2,1,0:T(8,128)(2,1)S(1)}, bf16[16,128,128]{2,1,0:T(8,128)(2,1)S(1)}, u32[]{:S(2)}, u32[]{:S(2)}) collective-permute-start(bf16[16,128,128]{2,1,0:T(8,128)(2,1)S(1)} %get-tuple-element.34), channel_id=1, source_target_pairs={{0,1},{1,2},{2,3},{3,4},{4,5},{5,6},{6,7},{7,0},{8,9},{9,10},{10,1... | collective-permute-start | bytes 1572872 | tf_op jit(solution)/shard_map/ppermute | solution.py:23
  204.0 14.2 %collective-permute-start.13 = (bf16[16,128,128]{2,1,0:T(8,128)(2,1)S(1)}, bf16[16,128,128]{2,1,0:T(8,128)(2,1)S(1)}, u32[]{:S(2)}, u32[]{:S(2)}) collective-permute-start(bf16[16,128,128]{2,1,0:T(8,128)(2,1)S(1)} %get-tuple-element.36), channel_id=1, source_target_pairs={{1,0},{2,1},{3,2},{4,3},{5,4},{6,5},{7,6},{0,7},{9,8},{10,9},{11,1... | collective-permute-start | bytes 1572872 | tf_op jit(solution)/shard_map/ppermute | solution.py:25
  204.6 13.7 %collective-permute-start.12 = (bf16[16,128,128]{2,1,0:T(8,128)(2,1)S(1)}, bf16[16,128,128]{2,1,0:T(8,128)(2,1)S(1)}, u32[]{:S(2)}, u32[]{:S(2)}) collective-permute-start(bf16[16,128,128]{2,1,0:T(8,128)(2,1)S(1)} %get-tuple-element.36), channel_id=1, source_target_pairs={{0,1},{1,2},{2,3},{3,4},{4,5},{5,6},{6,7},{7,0},{8,9},{9,10},{10,1... | collective-permute-start | bytes 1572872 | tf_op jit(solution)/shard_map/ppermute | solution.py:23
  246.5 14.2 %collective-permute-start.15 = (bf16[16,128,128]{2,1,0:T(8,128)(2,1)S(1)}, bf16[16,128,128]{2,1,0:T(8,128)(2,1)S(1)}, u32[]{:S(2)}, u32[]{:S(2)}) collective-permute-start(bf16[16,128,128]{2,1,0:T(8,128)(2,1)S(1)} %get-tuple-element.38), channel_id=1, source_target_pairs={{1,0},{2,1},{3,2},{4,3},{5,4},{6,5},{7,6},{0,7},{9,8},{10,9},{11,1... | collective-permute-start | bytes 1572872 | tf_op jit(solution)/shard_map/ppermute | solution.py:25
  246.5 14.2 %collective-permute-start.14 = (bf16[16,128,128]{2,1,0:T(8,128)(2,1)S(1)}, bf16[16,128,128]{2,1,0:T(8,128)(2,1)S(1)}, u32[]{:S(2)}, u32[]{:S(2)}) collective-permute-start(bf16[16,128,128]{2,1,0:T(8,128)(2,1)S(1)} %get-tuple-element.38), channel_id=1, source_target_pairs={{0,1},{1,2},{2,3},{3,4},{4,5},{5,6},{6,7},{7,0},{8,9},{9,10},{10,1... | collective-permute-start | bytes 1572872 | tf_op jit(solution)/shard_map/ppermute | solution.py:23
  288.9 14.2 %collective-permute-start.17 = (bf16[16,128,128]{2,1,0:T(8,128)(2,1)S(1)}, bf16[16,128,128]{2,1,0:T(8,128)(2,1)S(1)}, u32[]{:S(2)}, u32[]{:S(2)}) collective-permute-start(bf16[16,128,128]{2,1,0:T(8,128)(2,1)S(1)} %get-tuple-element.40), channel_id=1, source_target_pairs={{1,0},{2,1},{3,2},{4,3},{5,4},{6,5},{7,6},{0,7},{9,8},{10,9},{11,1... | collective-permute-start | bytes 1572872 | tf_op jit(solution)/shard_map/ppermute | solution.py:25
  288.9 14.2 %collective-permute-start.16 = (bf16[16,128,128]{2,1,0:T(8,128)(2,1)S(1)}, bf16[16,128,128]{2,1,0:T(8,128)(2,1)S(1)}, u32[]{:S(2)}, u32[]{:S(2)}) collective-permute-start(bf16[16,128,128]{2,1,0:T(8,128)(2,1)S(1)} %get-tuple-element.40), channel_id=1, source_target_pairs={{0,1},{1,2},{2,3},{3,4},{4,5},{5,6},{6,7},{7,0},{8,9},{9,10},{10,1... | collective-permute-start | bytes 1572872 | tf_op jit(solution)/shard_map/ppermute | solution.py:23
  335.9 4.4 collective-permute-start.19
  336.0 4.4 collective-permute-start.18
  342.9 7.5 %collective-permute-start.21 = (bf16[4,128,128]{2,0,1:T(4,128)(2,1)S(1)}, bf16[4,128,128]{2,0,1:T(4,128)(2,1)S(1)}, u32[]{:S(2)}, u32[]{:S(2)}) collective-permute-start(bf16[4,128,128]{2,0,1:T(4,128)(2,1)S(1)} %get-tuple-element.5), channel_id=1, source_target_pairs={{1,0},{2,1},{3,2},{4,3},{5,4},{6,5},{7,6},{0,7},{9,8},{10,9},{11,1... | collective-permute-start | bytes 393224 | tf_op jit(solution)/shard_map/ppermute | solution.py:25
  356.5 15.0 %collective-permute-start.23 = (bf16[16,128,128]{2,1,0:T(8,128)(2,1)S(1)}, bf16[16,128,128]{2,1,0:T(8,128)(2,1)S(1)}, u32[]{:S(2)}, u32[]{:S(2)}) collective-permute-start(bf16[16,128,128]{2,1,0:T(8,128)(2,1)S(1)} %fusion.45), channel_id=1, source_target_pairs={{1,0},{2,1},{3,2},{4,3},{5,4},{6,5},{7,6},{0,7},{9,8},{10,9},{11,1... | collective-permute-start | bytes 1572872 | tf_op jit(solution)/shard_map/ppermute | solution.py:25
  359.6 11.9 %collective-permute-start.22 = (bf16[16,128,128]{2,1,0:T(8,128)(2,1)S(1)}, bf16[16,128,128]{2,1,0:T(8,128)(2,1)S(1)}, u32[]{:S(2)}, u32[]{:S(2)}) collective-permute-start(bf16[16,128,128]{2,1,0:T(8,128)(2,1)S(1)} %fusion.45), channel_id=1, source_target_pairs={{0,1},{1,2},{2,3},{3,4},{4,5},{5,6},{6,7},{7,0},{8,9},{9,10},{10,1... | collective-permute-start | bytes 1572872 | tf_op jit(solution)/shard_map/ppermute | solution.py:23
  400.1 14.2 %collective-permute-start.25 = (bf16[16,128,128]{2,1,0:T(8,128)(2,1)S(1)}, bf16[16,128,128]{2,1,0:T(8,128)(2,1)S(1)}, u32[]{:S(2)}, u32[]{:S(2)}) collective-permute-start(bf16[16,128,128]{2,1,0:T(8,128)(2,1)S(1)} %get-tuple-element.43), channel_id=1, source_target_pairs={{1,0},{2,1},{3,2},{4,3},{5,4},{6,5},{7,6},{0,7},{9,8},{10,9},{11,1... | collective-permute-start | bytes 1572872 | tf_op jit(solution)/shard_map/ppermute | solution.py:25
  400.4 14.0 %collective-permute-start.24 = (bf16[16,128,128]{2,1,0:T(8,128)(2,1)S(1)}, bf16[16,128,128]{2,1,0:T(8,128)(2,1)S(1)}, u32[]{:S(2)}, u32[]{:S(2)}) collective-permute-start(bf16[16,128,128]{2,1,0:T(8,128)(2,1)S(1)} %get-tuple-element.43), channel_id=1, source_target_pairs={{0,1},{1,2},{2,3},{3,4},{4,5},{5,6},{6,7},{7,0},{8,9},{9,10},{10,1... | collective-permute-start | bytes 1572872 | tf_op jit(solution)/shard_map/ppermute | solution.py:23
  (13 other events, 204.5 us)
where the time goes:
time: 452 us; the launch traced here: 445 us
  matrix products  150 us (33%)
  local copies, waits for them, and re-layouts  129 us (29%)
  waiting for transfers between devices  98.1 us (22%)
  starting transfers between devices  41.5 us (9%)
  blocking collectives  14.4 us (3%)
  other arithmetic  11.9 us (3%)
    dot_general x9, matrix products, fine_apply(): jnp.einsum('rkij,rkjn->rin', fine_blocks, gathered, preferred_element_typ...  136 us
    gather x9, local copies, waits for them, and re-layouts, fine_apply(): gathered = extended[local_index]  125 us
    ppermute x13, waiting for transfers between devices, with_halo(): lax.ppermute(head, axis, [((i + 1) % count, i) for i in range(count)])  89.4 us
    ppermute x13, starting transfers between devices, with_halo(): lax.ppermute(head, axis, [((i + 1) % count, i) for i in range(count)])  28.1 us
    ppermute x13, starting transfers between devices, with_halo(): lax.ppermute(tail, axis, [(i, (i + 1) % count) for i in range(count)])  13.4 us
  transfers between devices with their start and end apart: 26, of which 15 were waited for; matrix products, arithmetic and copies ran while one was open for 1% of the time, Pallas kernels for 0%

commit v1 on v0

v1 whole, which is shorter than its diff:
```python
import functools

import jax
import jax.numpy as jnp
from jax import lax
from jax.experimental import pallas as pl
from jax.experimental.pallas import tpu as pltpu
from jax.sharding import PartitionSpec as P

CYCLES = 2
SWEEPS = 2
CHEB = 3
relax_weight = 0.7
centre = 1.0
half_width = 0.6

PARTS = 4
STAGES = 4
MESH = pl.DeviceIdType.MESH
F32 = jnp.float32
BF16 = jnp.bfloat16


def kernel(
    geo,
    table,
    source_ref,
    blocks_ref,
    diag_ref,
    mask_ref,
    coarse_ref,
    cdiag_ref,
    out_ref,
    *scratch,
):
    n_rows, n_rhs, block_rows, stored, size = geo
    stages = scratch[:STAGES]
    (
        band,
        xown,
        xleft,
        xright,
        acc,
        rhs,
        weight,
        diag,
        lmask,
        rmask,
        cops,
        cdiags,
        cinv,
        csource,
        ccorr,
        cupd,
        csend,
        lrim,
        rrim,
        stage_sem,
        fsend_sem,
        frecv_sem,
        csend_sem,
        crecv_sem,
        msend_sem,
        mrecv_sem,
        gsend_sem,
        grecv_sem,
    ) = scratch[STAGES:]
    per = block_rows // PARTS
    part = per * size
    groups = n_rhs
    wide = stored + per
    me = lax.axis_index("rows")
    mine = lax.axis_index("rhs")
    right = lax.rem(me + 1, n_rows)
    left = lax.rem(me + n_rows - 1, n_rows)
    low_shift = (me + n_rows - 1) // n_rows
    high_shift = (me + 1) // n_rows

    def stage_copy(row, s):
        return pltpu.make_async_copy(
            blocks_ref.at[row], stages[s].at[pl.ds(0, stored)], stage_sem.at[s]
        )

    for s in range(STAGES):
        stage_copy(s, s).start()

    barrier = pltpu.get_barrier_semaphore()
    for other in (left, right):
        pl.semaphore_signal(barrier, inc=1, device_id={"rows": other}, device_id_type=MESH)
    for step in range(1, n_rhs):
        peer = lax.rem(mine + step, n_rhs)
        pl.semaphore_signal(barrier, inc=1, device_id={"rhs": peer}, device_id_type=MESH)

    for r in range(block_rows):
        rows = pl.ds(r * size, size)
        column = jnp.broadcast_to(diag_ref[pl.ds(r, 1), :], (size, size)).T
        diag[rows, :] = column
        scale = relax_weight / column
        weight[rows, :] = scale
        value = source_ref[rows, :]
        rhs[0, rows, :] = value
        value = scale * value
        out_ref[rows, :] = value
        xown[0, r // per, pl.ds((r % per) * size, size), :] = value.astype(BF16)
    cops[mine] = coarse_ref[...].astype(BF16)
    cdiags[mine] = cdiag_ref[...]
    zero = jnp.zeros((size, size), BF16)
    for s in range(STAGES):
        stages[s][stored] = zero
    for t in range(CHEB):
        lrim[t, 0] = zero
        rrim[t, groups] = zero
    pl.semaphore_wait(barrier, n_rhs + 1)

    def fine_copy(way, slot, c):
        return pltpu.make_async_remote_copy(
            src_ref=xown.at[slot, c],
            dst_ref=(xleft if way == 0 else xright).at[slot, c],
            send_sem=fsend_sem.at[way, slot, c],
            recv_sem=frecv_sem.at[way, slot, c],
            device_id={"rows": right if way == 0 else left},
            device_id_type=MESH,
        )

    def coarse_copy(way, t):
        return pltpu.make_async_remote_copy(
            src_ref=csend.at[t],
            dst_ref=lrim.at[t, pl.ds(1, groups)] if way == 0 else rrim.at[t, pl.ds(0, groups)],
            send_sem=csend_sem.at[way, t],
            recv_sem=crecv_sem.at[way, t],
            device_id={"rows": right if way == 0 else left},
            device_id_type=MESH,
        )

    def mask_copy(way):
        return pltpu.make_async_remote_copy(
            src_ref=mask_ref,
            dst_ref=lmask if way == 0 else rmask,
            send_sem=msend_sem.at[way],
            recv_sem=mrecv_sem.at[way],
            device_id={"rows": right if way == 0 else left},
            device_id_type=MESH,
        )

    def gather_copies(step):
        peer = lax.rem(mine + step, n_rhs)
        return [
            pltpu.make_async_remote_copy(
                src_ref=whole.at[mine],
                dst_ref=whole.at[mine],
                send_sem=gsend_sem.at[k, step - 1],
                recv_sem=grecv_sem.at[k, step - 1],
                device_id={"rhs": peer},
                device_id_type=MESH,
            )
            for k, whole in enumerate((cops, cdiags))
        ]

    middle = list(range(1, PARTS - 1))

    def send_part(slot, c):
        fine_copy(0, slot, c).start()
        fine_copy(1, slot, c).start()

    for c in middle:
        send_part(0, c)
    fine_copy(0, 0, PARTS - 1).start()
    fine_copy(1, 0, 0).start()
    fine_copy(0, 0, 0).start()
    fine_copy(1, 0, PARTS - 1).start()
    for way in (0, 1):
        mask_copy(way).start()
    for step in range(1, n_rhs):
        for copy in gather_copies(step):
            copy.start()

    rounds = block_rows // STAGES

    def lay(turn, carry):
        for s in range(STAGES):
            row = turn * STAGES + s
            stage_copy(row, s).wait()
            rows = pl.ds(pl.multiple_of(row * size, size), size)
            for j in range(wide):
                band[rows, pl.ds(j * size, size)] = stages[s][table[row * wide + j]]

            @pl.when(turn < rounds - 1)
            def _():
                stage_copy(row + STAGES, s).start()

        return carry

    lax.fori_loop(0, rounds, lay, 0)

    for way in (0, 1):
        mask_copy(way).wait()
    for step in range(1, n_rhs):
        for copy in gather_copies(step):
            copy.wait()
    for q in range(groups):
        row = cdiags[q][0:1, :]
        cinv[q] = 1.0 / jnp.broadcast_to(row, (size, size)).T

    def rows_of(g):
        return pl.ds(g * part, part)

    def times(g, first, count, x):
        lhs = band[rows_of(g), pl.ds(first * part, count * part)]
        return jnp.dot(lhs, x, preferred_element_type=F32)

    def spread(marks, l, fields):
        total = None
        for q in range(groups):
            term = marks[pl.ds(l * groups + q, 1), :] * fields[q].astype(F32)
            total = term if total is None else total + term
        return total

    def coarse_solve(slot):
        for q in range(groups):
            total = jnp.zeros((size, size), F32)
            for r in range(block_rows):
                total += mask_ref[pl.ds(r * groups + q, 1), :] * rhs[1, pl.ds(r * size, size), :]
            csource[q] = total
            first = total * cinv[q] / centre
            cupd[q] = first
            ccorr[q] = first
            csend[0, q] = first.astype(BF16)
        coarse_copy(0, 0).start()
        coarse_copy(1, 0).start()
        sigma = centre / half_width
        old = 1.0 / sigma
        for t in range(CHEB - 1):
            new = 1.0 / (2.0 * sigma - old)
            for q in range(groups):
                acc[pl.ds(q * size, size), :] = jnp.dot(
                    cops[q, 1], csend[t, q], preferred_element_type=F32
                )
            coarse_copy(0, t).wait_recv()
            coarse_copy(1, t).wait_recv()
            for q in range(groups):
                value = acc[pl.ds(q * size, size), :]
                value += jnp.dot(cops[q, 0], lrim[t, q + low_shift], preferred_element_type=F32)
                value += jnp.dot(cops[q, 2], rrim[t, q + high_shift], preferred_element_type=F32)
                corr = ccorr[q]
                scaled = (csource[q] - value) * cinv[q] - corr
                update = new * old * cupd[q] + (2.0 * new / half_width) * scaled
                corr = corr + update
                cupd[q] = update
                ccorr[q] = corr
                csend[t + 1, q] = corr.astype(BF16)
            coarse_copy(0, t + 1).start()
            coarse_copy(1, t + 1).start()
            old = new
        fields = [ccorr.at[q] for q in range(groups)]
        for r in range(block_rows):
            rows = pl.ds(r * size, size)
            value = spread(mask_ref, r, [f[...] for f in fields])
            out_ref[rows, :] = out_ref[rows, :] + (1.0 - relax_weight) * value
            xown[slot, r // per, pl.ds((r % per) * size, size), :] = value.astype(BF16)

    applies = CYCLES * (2 * SWEEPS + 1) - 1
    turn_len = 2 * SWEEPS + 1

    def apply(e, carry):
        slot = lax.rem(e, 2)
        after = 1 - slot
        place = lax.rem(e + 1, turn_len)
        is_residual = place == SWEEPS
        is_first_post = place == SWEEPS + 1
        keep = jnp.where(is_first_post, 1.0, 1.0 - relax_weight).astype(F32)
        side = jnp.where(is_first_post, 1, 0)

        own = xown[slot].reshape(PARTS * part, size)
        for g in range(PARTS):
            acc[rows_of(g), :] = times(g, PARTS - g, PARTS, own)

        @pl.when(is_first_post)
        def _():
            t = CHEB - 1
            for way in (0, 1):
                coarse_copy(way, t).wait_recv()
                rim, marks, halo = ((lrim, lmask, xleft), (rrim, rmask, xright))[way]
                first = 1 if way == 0 else 0
                for r in range(block_rows):
                    value = spread(marks, r, [rim[t, first + q] for q in range(groups)])
                    halo[slot, r // per, pl.ds((r % per) * size, size), :] = value.astype(BF16)
                for k in range(CHEB):
                    coarse_copy(way, k).wait_send()

        def await_part(way, c):
            @pl.when(jnp.logical_not(is_first_post))
            def _():
                fine_copy(way, slot, c).wait_recv()

        def add_left(c):
            await_part(0, c)
            x = xleft[slot, c]
            for g in range(c + 1):
                acc[rows_of(g), :] += times(g, c - g, 1, x)

        def add_right(c):
            await_part(1, c)
            x = xright[slot, c]
            for g in range(c, PARTS):
                acc[rows_of(g), :] += times(g, 2 * PARTS + c - g, 1, x)

        def finish(g):
            rows = rows_of(g)

            @pl.when(is_residual)
            def _():
                rhs[1, rows, :] = rhs[0, rows, :] - diag[rows, :] * out_ref[rows, :] - acc[rows, :]

            @pl.when(jnp.logical_not(is_residual))
            def _():
                value = keep * out_ref[rows, :] + weight[rows, :] * (rhs[side, rows, :] - acc[rows, :])
                out_ref[rows, :] = value
                xown[after, g] = value.astype(BF16)

        sends = jnp.logical_and(jnp.logical_not(is_residual), e < applies - 1)
        for c in middle:
            add_right(c)
            add_left(PARTS - 1 - c)
        add_left(PARTS - 1)
        add_right(0)
        for g in middle:
            finish(g)

        @pl.when(sends)
        def _():
            for g in middle:
                send_part(after, g)

        add_left(0)
        add_right(PARTS - 1)
        finish(PARTS - 1)
        finish(0)

        @pl.when(sends)
        def _():
            fine_copy(0, after, PARTS - 1).start()
            fine_copy(1, after, 0).start()
            fine_copy(0, after, 0).start()
            fine_copy(1, after, PARTS - 1).start()

        @pl.when(jnp.logical_not(is_first_post))
        def _():
            for way in (0, 1):
                for c in range(PARTS):
                    fine_copy(way, slot, c).wait_send()

        @pl.when(is_residual)
        def _():
            coarse_solve(after)

        return carry

    lax.fori_loop(0, applies, apply, 0)


def shards(right_side, fine_blocks, fine_columns, fine_diag, aggregate, coarse_blocks, coarse_diag):
    block_rows, stored, size, _ = fine_blocks.shape
    n_rows = lax.axis_size("rows")
    n_rhs = lax.axis_size("rhs")
    total_blocks = block_rows * n_rows
    groups = n_rhs * coarse_blocks.shape[0]
    per = block_rows // PARTS
    part = per * size
    wide = stored + per
    reach = stored // 2

    local = jnp.arange(block_rows, dtype=jnp.int32)[:, None]
    first = lax.axis_index("rows") * block_rows
    places = jnp.mod(fine_columns - (first + local) + reach, total_blocks) + local % per
    hit = places[:, None, :] == jnp.arange(wide, dtype=jnp.int32)[None, :, None]
    order = jnp.arange(stored, dtype=jnp.int32)[None, None, :]
    found = jnp.max(jnp.where(hit, order, -1), axis=2)
    table = jnp.where(found < 0, stored, found).reshape(block_rows * wide)

    group_id = aggregate // n_rows
    marks = (group_id[:, None] == jnp.arange(groups, dtype=jnp.int32)[None, :]).astype(F32)
    marks = jnp.broadcast_to(marks[:, :, None], (block_rows, groups, size))
    marks = marks.reshape(block_rows * groups, size)
    coarse_rows = jnp.broadcast_to(coarse_diag[None, :], (8, size))

    vmem = pl.BlockSpec(memory_space=pltpu.VMEM)
    field = PARTS * part
    geo = (n_rows, n_rhs, block_rows, stored, size)
    return pl.pallas_call(
        functools.partial(kernel, geo),
        out_shape=jax.ShapeDtypeStruct((field, size), F32),
        in_specs=[
            pl.BlockSpec(memory_space=pltpu.SMEM),
            vmem,
            pl.BlockSpec(memory_space=pl.ANY),
            vmem,
            vmem,
            vmem,
            vmem,
        ],
        out_specs=vmem,
        scratch_shapes=[pltpu.VMEM((stored + 1, size, size), BF16) for _ in range(STAGES)]
        + [
            pltpu.VMEM((field, wide * size), BF16),
            pltpu.VMEM((2, PARTS, part, size), BF16),
            pltpu.VMEM((2, PARTS, part, size), BF16),
            pltpu.VMEM((2, PARTS, part, size), BF16),
            pltpu.VMEM((field, size), F32),
            pltpu.VMEM((2, field, size), F32),
            pltpu.VMEM((field, size), F32),
            pltpu.VMEM((field, size), F32),
            pltpu.VMEM((block_rows * groups, size), F32),
            pltpu.VMEM((block_rows * groups, size), F32),
            pltpu.VMEM((groups, 3, size, size), BF16),
            pltpu.VMEM((groups, 8, size), F32),
            pltpu.VMEM((groups, size, size), F32),
            pltpu.VMEM((groups, size, size), F32),
            pltpu.VMEM((groups, size, size), F32),
            pltpu.VMEM((groups, size, size), F32),
            pltpu.VMEM((CHEB, groups, size, size), BF16),
            pltpu.VMEM((CHEB, groups + 1, size, size), BF16),
            pltpu.VMEM((CHEB, groups + 1, size, size), BF16),
            pltpu.SemaphoreType.DMA((STAGES,)),
            pltpu.SemaphoreType.DMA((2, 2, PARTS)),
            pltpu.SemaphoreType.DMA((2, 2, PARTS)),
            pltpu.SemaphoreType.DMA((2, CHEB)),
            pltpu.SemaphoreType.DMA((2, CHEB)),
            pltpu.SemaphoreType.DMA((2,)),
            pltpu.SemaphoreType.DMA((2,)),
            pltpu.SemaphoreType.DMA((2, n_rhs - 1)),
            pltpu.SemaphoreType.DMA((2, n_rhs - 1)),
        ],
        compiler_params=pltpu.CompilerParams(
            collective_id=0, has_side_effects=True, vmem_limit_bytes=56 * 1024 * 1024
        ),
    )(
        table,
        right_side,
        fine_blocks,
        fine_diag.reshape(block_rows, size),
        marks,
        coarse_blocks[0],
        coarse_rows,
    )


def solution(mesh):
    in_specs = (
        P("rows", "rhs"),
        P("rows", None, None, None),
        P("rows", None),
        P("rows"),
        P("rows"),
        P(("rhs", "rows"), None, None, None),
        P(("rhs", "rows")),
    )
    out_specs = P("rows", "rhs")
    return jax.shard_map(shards, mesh=mesh, in_specs=in_specs, out_specs=out_specs, check_vma=False)
```

time: 452 us -> 146 us (0.32); the launches traced: 445 us -> 146 us
  matrix products: 150 us -> 0 us
  Pallas kernels: 0 us -> 139 us
  local copies, waits for them, and re-layouts: 129 us -> 4.37 us
  waiting for transfers between devices: 98.1 us -> 0 us
  starting transfers between devices: 41.5 us -> 0 us
  blocking collectives: 14.4 us -> 0 us
  other arithmetic: 11.9 us -> 2.26 us
    dot_general x25 -> x0, matrix products: 150 us -> none  [the longest x9 136 us: fine_apply(): jnp.einsum('rkij,rkjn->rin', fine_blocks, gathered, preferred_element_typ...]
    pallas_call x0 -> x1, Pallas kernels: none -> 139 us  [shards(): pl.pallas_call(functools.partial(kernel, geo), out_shape=jax.ShapeDtypeSt...]
    gather x9 -> x0, local copies, waits for them, and re-layouts: 125 us -> none  [fine_apply(): gathered = extended[local_index]]
    ppermute x26 -> x0, waiting for transfers between devices: 98.1 us -> none  [the longest x13 89.4 us: with_halo(): lax.ppermute(head, axis, [((i + 1) % count, i) for i in range(count)])]
    ppermute x26 -> x0, starting transfers between devices: 41.5 us -> none  [the longest x13 28.1 us: with_halo(): lax.ppermute(head, axis, [((i + 1) % count, i) for i in range(count)])]
    all_gather x2 -> x0, blocking collectives: 14.4 us -> none  [the longest x1 8.14 us: shards(): lax.all_gather(coarse_blocks.astype(jnp.bfloat16), 'rhs', axis=0, tiled=T...]
    convert_element_type x10 -> x1, other arithmetic: 6.1 us -> 0.07 us  [shards(): (group_id[:, None] == jnp.arange(groups, dtype=jnp.int32)[None, :]).astyp...]
  transfers between devices with their start and end apart: 26 -> 0, of which waited for: 15 -> 0; matrix products, arithmetic and copies ran while one was open for 1% -> 0% of each run, Pallas kernels for 0% -> 0%
where the time goes in v1:
time: 146 us
  Pallas kernels  139 us (95%)
  local copies, waits for them, and re-layouts  4.37 us (3%)
  other arithmetic  2.26 us (2%)
    pallas_call x1, Pallas kernels, shards(): pl.pallas_call(functools.partial(kernel, geo), out_shape=jax.ShapeDtypeSt...  139 us

profile of v1, /device:TPU:1, one launch (start us, length us, event | category | flops | bytes accessed | tf_op | source)
XLA Modules:
  0.0 146.1 jit_solution(11540807157551972264)
XLA Ops:
  0.0 0.7 and_select_fusion
  0.7 1.2 broadcast_in_dim.38.cdiag_ref
  1.9 0.8 fusion.1
  2.7 0.2 select_reduce_fusion
  2.9 0.1 reduce_max.12
  2.9 0.6 compare_select_fusion.table
  3.5 0.1 fusion.2
  3.6 0.1 reshape.53
  3.7 0.7 broadcast_in_dim.23.mask_ref
  4.4 139.4 %shard_map.73 = f32[2048,128]{1,0:T(8,128)} custom-call(s32[576]{0:T(1024)} %compare_select_fusion.table, f32[2048,128]{1,0:T(8,128)} %source_ref.1, bf16[16,32,128,128]{3,2,1,0:T(8,128)(2,1)} %blocks_ref.1, f32[16,128]{1,0:T(8,128)} %bitcast.3, f32[64,128]{1,0:T(8,128)} %broadcast_in_dim.23.mask_ref, f32[3,128,128]{2,1,0:T(8,128)} %bitcast.2, ...), custom_call_target="tpu_custom_call" | custom-call | tf_op jit(solution)/shard_map/pallas_call | solution.py:389
  143.8 2.3 %copy.9 = f32[2048,128]{1,0:T(8,128)} copy(f32[2048,128]{1,0:T(8,128)} %shard_map.73) | data formatting | bytes 2097152
  (1 shorter events, 0.0 us)

commit v2 on v1

--- a/solution.py
+++ b/solution.py
@@ -27,7 +27,7 @@
     source_ref,
     blocks_ref,
     diag_ref,
-    mask_ref,
+    aggregate_ref,
     coarse_ref,
     cdiag_ref,
     out_ref,
@@ -46,6 +46,7 @@
         diag,
         lmask,
         rmask,
+        mask_ref,
         cops,
         cdiags,
         cinv,
@@ -91,27 +92,6 @@
         peer = lax.rem(mine + step, n_rhs)
         pl.semaphore_signal(barrier, inc=1, device_id={"rhs": peer}, device_id_type=MESH)
 
-    for r in range(block_rows):
-        rows = pl.ds(r * size, size)
-        column = jnp.broadcast_to(diag_ref[pl.ds(r, 1), :], (size, size)).T
-        diag[rows, :] = column
-        scale = relax_weight / column
-        weight[rows, :] = scale
-        value = source_ref[rows, :]
-        rhs[0, rows, :] = value
-        value = scale * value
-        out_ref[rows, :] = value
-        xown[0, r // per, pl.ds((r % per) * size, size), :] = value.astype(BF16)
-    cops[mine] = coarse_ref[...].astype(BF16)
-    cdiags[mine] = cdiag_ref[...]
-    zero = jnp.zeros((size, size), BF16)
-    for s in range(STAGES):
-        stages[s][stored] = zero
-    for t in range(CHEB):
-        lrim[t, 0] = zero
-        rrim[t, groups] = zero
-    pl.semaphore_wait(barrier, n_rhs + 1)
-
     def fine_copy(way, slot, c):
         return pltpu.make_async_remote_copy(
             src_ref=xown.at[slot, c],
@@ -122,12 +102,12 @@
             device_id_type=MESH,
         )
 
-    def coarse_copy(way, t):
+    def coarse_copy(way, t, q):
         return pltpu.make_async_remote_copy(
-            src_ref=csend.at[t],
-            dst_ref=lrim.at[t, pl.ds(1, groups)] if way == 0 else rrim.at[t, pl.ds(0, groups)],
-            send_sem=csend_sem.at[way, t],
-            recv_sem=crecv_sem.at[way, t],
+            src_ref=csend.at[t, q],
+            dst_ref=lrim.at[t, 1 + q] if way == 0 else rrim.at[t, q],
+            send_sem=csend_sem.at[way, t, q],
+            recv_sem=crecv_sem.at[way, t, q],
             device_id={"rows": right if way == 0 else left},
             device_id_type=MESH,
         )
@@ -162,17 +142,48 @@
         fine_copy(0, slot, c).start()
         fine_copy(1, slot, c).start()
 
+    def begin(c):
+        for r in range(c * per, (c + 1) * per):
+            rows = pl.ds(r * size, size)
+            column = jnp.broadcast_to(diag_ref[pl.ds(r, 1), :], (size, size)).T
+            diag[rows, :] = column
+            scale = relax_weight / column
+            weight[rows, :] = scale
+            value = source_ref[rows, :]
+            rhs[0, rows, :] = value
+            value = scale * value
+            out_ref[rows, :] = value
+            xown[0, c, pl.ds((r % per) * size, size), :] = value.astype(BF16)
+
+    for c in middle:
+        begin(c)
+    pl.semaphore_wait(barrier, n_rhs + 1)
     for c in middle:
         send_part(0, c)
+    begin(PARTS - 1)
+    begin(0)
     fine_copy(0, 0, PARTS - 1).start()
     fine_copy(1, 0, 0).start()
     fine_copy(0, 0, 0).start()
     fine_copy(1, 0, PARTS - 1).start()
-    for way in (0, 1):
-        mask_copy(way).start()
+
+    cops[mine] = coarse_ref[...].astype(BF16)
+    cdiags[mine] = jnp.broadcast_to(cdiag_ref[...], (8, size))
     for step in range(1, n_rhs):
         for copy in gather_copies(step):
             copy.start()
+    zero = jnp.zeros((size, size), BF16)
+    for s in range(STAGES):
+        stages[s][stored] = zero
+    for t in range(CHEB):
+        lrim[t, 0] = zero
+        rrim[t, groups] = zero
+    for r in range(block_rows):
+        for q in range(groups):
+            mark = jnp.where(aggregate_ref[r] == q * n_rows + me, 1.0, 0.0).astype(F32)
+            mask_ref[pl.ds(r * groups + q, 1), :] = jnp.full((1, size), mark, F32)
+    for way in (0, 1):
+        mask_copy(way).start()
 
     rounds = block_rows // STAGES
 
@@ -225,8 +236,8 @@
             cupd[q] = first
             ccorr[q] = first
             csend[0, q] = first.astype(BF16)
-        coarse_copy(0, 0).start()
-        coarse_copy(1, 0).start()
+            coarse_copy(0, 0, q).start()
+            coarse_copy(1, 0, q).start()
         sigma = centre / half_width
         old = 1.0 / sigma
         for t in range(CHEB - 1):
@@ -235,9 +246,11 @@
                 acc[pl.ds(q * size, size), :] = jnp.dot(
                     cops[q, 1], csend[t, q], preferred_element_type=F32
                 )
-            coarse_copy(0, t).wait_recv()
-            coarse_copy(1, t).wait_recv()
+            coarse_copy(1, t, 0).wait_recv()
             for q in range(groups):
+                coarse_copy(0, t, q).wait_recv()
+                if q + 1 < groups:
+                    coarse_copy(1, t, q + 1).wait_recv()
                 value = acc[pl.ds(q * size, size), :]
                 value += jnp.dot(cops[q, 0], lrim[t, q + low_shift], preferred_element_type=F32)
                 value += jnp.dot(cops[q, 2], rrim[t, q + high_shift], preferred_element_type=F32)
@@ -248,8 +261,8 @@
                 cupd[q] = update
                 ccorr[q] = corr
                 csend[t + 1, q] = corr.astype(BF16)
-            coarse_copy(0, t + 1).start()
-            coarse_copy(1, t + 1).start()
+                coarse_copy(0, t + 1, q).start()
+                coarse_copy(1, t + 1, q).start()
             old = new
         fields = [ccorr.at[q] for q in range(groups)]
         for r in range(block_rows):
@@ -274,77 +287,87 @@
         for g in range(PARTS):
             acc[rows_of(g), :] = times(g, PARTS - g, PARTS, own)
 
+        def relax(g):
+            rows = rows_of(g)
+            value = keep * out_ref[rows, :] + weight[rows, :] * (rhs[side, rows, :] - acc[rows, :])
+            out_ref[rows, :] = value
+            xown[after, g] = value.astype(BF16)
+
         @pl.when(is_first_post)
         def _():
             t = CHEB - 1
             for way in (0, 1):
-                coarse_copy(way, t).wait_recv()
                 rim, marks, halo = ((lrim, lmask, xleft), (rrim, rmask, xright))[way]
                 first = 1 if way == 0 else 0
+                for q in range(groups):
+                    coarse_copy(way, t, q).wait_recv()
                 for r in range(block_rows):
                     value = spread(marks, r, [rim[t, first + q] for q in range(groups)])
                     halo[slot, r // per, pl.ds((r % per) * size, size), :] = value.astype(BF16)
+            for g in middle + [PARTS - 1, 0]:
+                lower = xleft[slot, pl.ds(g, PARTS - g)].reshape((PARTS - g) * part, size)
+                upper = xright[slot, pl.ds(0, g + 1)].reshape((g + 1) * part, size)
+                acc[rows_of(g), :] += times(g, 0, PARTS - g, lower) + times(
+                    g, 2 * PARTS - g, g + 1, upper
+                )
+                relax(g)
+                send_part(after, g)
+            for way in (0, 1):
                 for k in range(CHEB):
-                    coarse_copy(way, k).wait_send()
-
-        def await_part(way, c):
-            @pl.when(jnp.logical_not(is_first_post))
-            def _():
-                fine_copy(way, slot, c).wait_recv()
-
-        def add_left(c):
-            await_part(0, c)
-            x = xleft[slot, c]
-            for g in range(c + 1):
-                acc[rows_of(g), :] += times(g, c - g, 1, x)
-
-        def add_right(c):
-            await_part(1, c)
-            x = xright[slot, c]
-            for g in range(c, PARTS):
-                acc[rows_of(g), :] += times(g, 2 * PARTS + c - g, 1, x)
-
-        def finish(g):
-            rows = rows_of(g)
-
-            @pl.when(is_residual)
-            def _():
-                rhs[1, rows, :] = rhs[0, rows, :] - diag[rows, :] * out_ref[rows, :] - acc[rows, :]
-
-            @pl.when(jnp.logical_not(is_residual))
-            def _():
-                value = keep * out_ref[rows, :] + weight[rows, :] * (rhs[side, rows, :] - acc[rows, :])
-                out_ref[rows, :] = value
-                xown[after, g] = value.astype(BF16)
-
-        sends = jnp.logical_and(jnp.logical_not(is_residual), e < applies - 1)
-        for c in middle:
-            add_right(c)
-            add_left(PARTS - 1 - c)
-        add_left(PARTS - 1)
-        add_right(0)
-        for g in middle:
-            finish(g)
-
-        @pl.when(sends)
-        def _():
-            for g in middle:
-                send_part(after, g)
-
-        add_left(0)
-        add_right(PARTS - 1)
-        finish(PARTS - 1)
-        finish(0)
-
-        @pl.when(sends)
-        def _():
-            fine_copy(0, after, PARTS - 1).start()
-            fine_copy(1, after, 0).start()
-            fine_copy(0, after, 0).start()
-            fine_copy(1, after, PARTS - 1).start()
+                    for q in range(groups):
+                        coarse_copy(way, k, q).wait_send()
 
         @pl.when(jnp.logical_not(is_first_post))
         def _():
+            def add_left(c):
+                fine_copy(0, slot, c).wait_recv()
+                x = xleft[slot, c]
+                for g in range(c + 1):
+                    acc[rows_of(g), :] += times(g, c - g, 1, x)
+
+            def add_right(c):
+                fine_copy(1, slot, c).wait_recv()
+                x = xright[slot, c]
+                for g in range(c, PARTS):
+                    acc[rows_of(g), :] += times(g, 2 * PARTS + c - g, 1, x)
+
+            def finish(g):
+                rows = rows_of(g)
+
+                @pl.when(is_residual)
+                def _():
+                    rhs[1, rows, :] = rhs[0, rows, :] - diag[rows, :] * out_ref[rows, :] - acc[rows, :]
+
+                @pl.when(jnp.logical_not(is_residual))
+                def _():
+                    relax(g)
+
+            sends = jnp.logical_and(jnp.logical_not(is_residual), e < applies - 1)
+            for c in middle:
+                add_right(c)
+                add_left(PARTS - 1 - c)
+            add_left(PARTS - 1)
+            add_right(0)
+            for g in middle:
+                finish(g)
+
+            @pl.when(sends)
+            def _():
+                for g in middle:
+                    send_part(after, g)
+
+            add_left(0)
+            add_right(PARTS - 1)
+            finish(PARTS - 1)
+            finish(0)
+
+            @pl.when(sends)
+            def _():
+                fine_copy(0, after, PARTS - 1).start()
+                fine_copy(1, after, 0).start()
+                fine_copy(0, after, 0).start()
+                fine_copy(1, after, PARTS - 1).start()
+
             for way in (0, 1):
                 for c in range(PARTS):
                     fine_copy(way, slot, c).wait_send()
@@ -376,12 +399,6 @@
     order = jnp.arange(stored, dtype=jnp.int32)[None, None, :]
     found = jnp.max(jnp.where(hit, order, -1), axis=2)
     table = jnp.where(found < 0, stored, found).reshape(block_rows * wide)
-
-    group_id = aggregate // n_rows
-    marks = (group_id[:, None] == jnp.arange(groups, dtype=jnp.int32)[None, :]).astype(F32)
-    marks = jnp.broadcast_to(marks[:, :, None], (block_rows, groups, size))
-    marks = marks.reshape(block_rows * groups, size)
-    coarse_rows = jnp.broadcast_to(coarse_diag[None, :], (8, size))
 
     vmem = pl.BlockSpec(memory_space=pltpu.VMEM)
     field = PARTS * part
@@ -394,7 +411,7 @@
             vmem,
             pl.BlockSpec(memory_space=pl.ANY),
             vmem,
-            vmem,
+            pl.BlockSpec(memory_space=pltpu.SMEM),
             vmem,
             vmem,
         ],
@@ -411,6 +428,7 @@
             pltpu.VMEM((field, size), F32),
             pltpu.VMEM((block_rows * groups, size), F32),
             pltpu.VMEM((block_rows * groups, size), F32),
+            pltpu.VMEM((block_rows * groups, size), F32),
             pltpu.VMEM((groups, 3, size, size), BF16),
             pltpu.VMEM((groups, 8, size), F32),
             pltpu.VMEM((groups, size, size), F32),
@@ -423,8 +441,8 @@
             pltpu.SemaphoreType.DMA((STAGES,)),
             pltpu.SemaphoreType.DMA((2, 2, PARTS)),
             pltpu.SemaphoreType.DMA((2, 2, PARTS)),
-            pltpu.SemaphoreType.DMA((2, CHEB)),
-            pltpu.SemaphoreType.DMA((2, CHEB)),
+            pltpu.SemaphoreType.DMA((2, CHEB, groups)),
+            pltpu.SemaphoreType.DMA((2, CHEB, groups)),
             pltpu.SemaphoreType.DMA((2,)),
             pltpu.SemaphoreType.DMA((2,)),
             pltpu.SemaphoreType.DMA((2, n_rhs - 1)),
@@ -438,9 +456,9 @@
         right_side,
         fine_blocks,
         fine_diag.reshape(block_rows, size),
-        marks,
+        aggregate,
         coarse_blocks[0],
-        coarse_rows,
+        coarse_diag.reshape(1, size),
     )
 
 

time: 146 us -> 136 us (0.932)
  Pallas kernels: 139 us -> 132 us
  local copies, waits for them, and re-layouts: 4.37 us -> 2.34 us
    pallas_call x1, Pallas kernels: 139 us -> 132 us  [shards(): pl.pallas_call(functools.partial(kernel, geo), out_shape=jax.ShapeDtypeSt...]
    broadcast_in_dim x2 -> x0, local copies, waits for them, and re-layouts: 1.94 us -> none  [the longest x1 1.25 us: shards(): coarse_rows = jnp.broadcast_to(coarse_diag[None, :], (8, size))]
where the time goes in v2:
time: 136 us
  Pallas kernels  132 us (97%)
  local copies, waits for them, and re-layouts  2.34 us (2%)
  other arithmetic  1.53 us (1%)
    pallas_call x1, Pallas kernels, shards(): pl.pallas_call(functools.partial(kernel, geo), out_shape=jax.ShapeDtypeSt...  132 us

profile of v2, /device:TPU:1, one launch (start us, length us, event | category | flops | bytes accessed | tf_op | source)
XLA Modules:
  0.0 135.9 jit_solution(13238343267879298382)
XLA Ops:
  0.0 0.8 fusion.1
  0.8 0.2 select_reduce_fusion
  0.9 0.1 reduce_max.12
  1.0 0.6 compare_select_fusion.table
  1.6 132.0 %shard_map.73 = f32[2048,128]{1,0:T(8,128)} custom-call(s32[576]{0:T(1024)} %compare_select_fusion.table, f32[2048,128]{1,0:T(8,128)} %source_ref.1, bf16[16,32,128,128]{3,2,1,0:T(8,128)(2,1)} %blocks_ref.1, f32[16,128]{1,0:T(8,128)} %bitcast.4, s32[16]{0:T(128)} %aggregate_ref.1, f32[3,128,128]{2,1,0:T(8,128)} %bitcast.3, f32[1,128]{1,0:T(1,128)} %bitcast.5), custom_call_target="tpu_custom_call" | custom-call | tf_op jit(solution)/shard_map/pallas_call | solution.py:406
  133.6 2.3 %copy.9 = f32[2048,128]{1,0:T(8,128)} copy(f32[2048,128]{1,0:T(8,128)} %shard_map.73) | data formatting | bytes 2097152
  (1 shorter events, 0.0 us)
